TPU v7x, 512 devices: a whole 4x4x16 slice. The times are simulated.
512 devices in a mesh: rep: 16 (over z_lo, x), fsdp: 32 (over z_hi, y, core).
Axes of the slice: x: 4, y: 4, z: 16 (z_hi: 4, z_lo: 4; z = z_hi * 4 + z_lo), core: 2. Of those that a mesh axis runs over, the one named last changes fastest.
Arguments:
- residual_in: bfloat16 [16, 12288, 2048], P('rep', 'fsdp'), may hold values from -6 to 6
- norm_gain: float32 [16, 2048], P('rep'), may hold values from 0.5 to 1.5
- kv_weight: bfloat16 [16, 2048, 1024], P('rep', 'fsdp'), may hold values from -0.125 to 0.125
- kv_grad: bfloat16 [16, 12288, 1024], P('rep', 'fsdp'), may hold values from -6 to 6
- outer_delta: float32 [16, 512, 2048], P('rep', 'fsdp'), may hold values from -6 to 6
- outer_momentum: float32 [512, 2048], P('fsdp'), may hold values from -6 to 6
- global_params: float32 [512, 2048], P('fsdp'), may hold values from -6 to 6
- sync_index: int32 [1], replicated, may hold values from 0 to 63
Outputs:
- grad_kv: bfloat16 [16, 2048, 1024], P('rep', 'fsdp')
- grad_gain: float32 [16, 2048], P('rep')
- grad_input: bfloat16 [16, 12288, 2048], P('rep', 'fsdp')
- new_params: float32 [512, 2048], P('fsdp')
- new_momentum: float32 [512, 2048], P('fsdp')
All inputs are finite; a program needn't handle non-finite values.
Results may differ from a plain program's by a relative error of at most 0.023.
Values may be sent and summed in bfloat16 or wider, within the bound.
A program may use at most 64 MiB of HBM per device.

v0:
```python
import jax
import jax.numpy as jnp
from jax import lax
from jax.sharding import PartitionSpec as P

ROUNDS = 64


EPSILON = 1e-05
NESTEROV_MU = 0.9
OUTER_RATE = 0.7


def inner_step(residual_in, norm_gain, kv_weight, kv_grad):
    resid = residual_in[0].astype(jnp.float32)
    gain_row = norm_gain[0]
    scale = lax.rsqrt(jnp.mean(resid * resid, axis=-1, keepdims=True) + EPSILON)
    unit = resid * scale
    normed = (unit * gain_row).astype(jnp.bfloat16)
    grads_here = kv_grad[0]
    contract_last = (((1,), (1,)), ((), ()))
    contract_first = (((0,), (0,)), ((), ()))
    grad_kv = lax.psum_scatter(
        lax.dot_general(
            normed, grads_here, contract_first, preferred_element_type=jnp.float32
        ).astype(jnp.bfloat16),
        "fsdp",
        scatter_dimension=0,
        tiled=True,
    )
    normed_grad = lax.dot_general(
        grads_here,
        lax.all_gather(kv_weight[0], "fsdp", axis=0, tiled=True),
        contract_last,
        preferred_element_type=jnp.float32,
    )
    grad_gain = lax.psum(jnp.sum(normed_grad * unit, axis=0), "fsdp")
    scaled = gain_row * normed_grad
    inner = jnp.mean(scaled * unit, axis=-1, keepdims=True)
    grad_input = (scale * (scaled - unit * inner)).astype(jnp.bfloat16)
    return (grad_kv[None], grad_gain[None], grad_input[None])


def nesterov(mean_delta, momentum, params, rate):
    fresh_momentum = NESTEROV_MU * momentum + mean_delta
    fresh_params = params - rate * (mean_delta + NESTEROV_MU * fresh_momentum)
    return (fresh_params, fresh_momentum)


def outer_step(outer_delta, outer_momentum, global_params, sync_index):
    replicas = lax.axis_size("rep")
    phase = sync_index[0].astype(jnp.float32) / ROUNDS
    rate = OUTER_RATE * (1.0 + jnp.cos(jnp.pi * phase)) / 2.0
    total = lax.psum(outer_delta[0].astype(jnp.bfloat16), "rep").astype(jnp.float32)
    return nesterov(total / replicas, outer_momentum, global_params, rate)


def local(
    residual_in,
    norm_gain,
    kv_weight,
    kv_grad,
    outer_delta,
    outer_momentum,
    global_params,
    sync_index,
):
    grad_kv, grad_gain, grad_input = inner_step(residual_in, norm_gain, kv_weight, kv_grad)
    new_params, new_momentum = outer_step(outer_delta, outer_momentum, global_params, sync_index)
    return (grad_kv, grad_gain, grad_input, new_params, new_momentum)


def solution(mesh):
    placed = (
        P("rep", "fsdp", None),
        P("rep", None),
        P("rep", "fsdp", None),
        P("rep", "fsdp", None),
        P("rep", "fsdp", None),
        P("fsdp", None),
        P("fsdp", None),
        P(),
    )
    return jax.shard_map(
        local,
        mesh=mesh,
        in_specs=placed,
        out_specs=(
            P("rep", "fsdp", None),
            P("rep", None),
            P("rep", "fsdp", None),
            P("fsdp", None),
            P("fsdp", None),
        ),
        check_vma=False,
    )
```

profile of v0, /device:TPU:1, one launch (start us, length us, event | category | flops | bytes accessed | tf_op | source)
XLA Modules:
  0.0 312.9 jit_solution(13156404719905392681)
XLA Ops:
  8.0 0.0 copy-start
  8.0 0.0 all-reduce.2.cloned.1.call-start
  8.1 1.6 convert_bitcast_fusion.1
  9.7 0.0 all-reduce.2.cloned.1.call-update
  9.7 0.0 all-gather.3.cloned.1.call-start
  9.7 0.5 all-gather.3.cloned.1.call-update
  10.3 0.0 reduce-scatter.2.cloned.1.call-start
  10.3 1.8 fusion.12
  12.1 0.0 copy-done
  12.1 5.8 %convolution_convert_fusion = bf16[2048,1024]{1,0:T(8,128)(2,1)} fusion(bf16[1,384,2048]{2,1,0:T(8,128)(2,1)} %param.8, f32[2048]{0:T(1024)} %bitcast.49, f32[384]{0:T(512)S(1)} %add_rsqrt_fusion, bf16[1,384,1024]{2,1,0:T(8,128)(2,1)S(1)} %copy-done), kind=kOutput, calls=%fused_computation.9 | convolution fusion | flops 1615855616 | bytes 6563328 | tf_op jit(solution)/shard_map/dot_general | solution.py:24
  17.9 0.0 copy-start.2
  17.9 0.0 copy-start.3
  17.9 0.0 copy-start.1
  17.9 0.0 copy-start.4
  18.0 0.0 reduce-scatter.2.cloned.1.call-update
  18.8 172.9 %all-reduce.2.cloned.1.call-done = bf16[16,2048]{1,0:T(8,128)(2,1)} async-done(((bf16[16,2048]{1,0:T(8,128)(2,1)}), bf16[16,2048]{1,0:T(8,128)(2,1)}) %all-reduce.2.cloned.1.call-update) | async-done | bytes 65552 | tf_op jit(solution)/shard_map/psum | solution.py:54
  191.7 0.0 copy-done.2
  191.7 0.0 copy-done.3
  191.7 1.6 multiply_subtract_fusion
  193.3 0.0 all-gather.3.cloned.1.call-done
  193.3 0.0 copy-done.1
  193.3 0.0 copy-done.4
  193.3 6.1 %fusion.8 = (f32[384]{0:T(512)S(1)}, f32[2048]{0:T(1024)S(1)}, f32[384,2048]{1,0:T(8,128)}) fusion(bf16[1,384,2048]{2,1,0:T(8,128)(2,1)S(1)} %copy-done.1, f32[2048]{0:T(1024)S(1)} %bitcast.50, f32[384]{0:T(512)S(1)} %add_rsqrt_fusion, bf16[1,2048,1024]{2,1,0:T(8,128)(2,1)} %all-gather.3.cloned.1.call-done, bf16[1,384,1024]{2,1,0:T(8,128)(2,1)S(1)} %copy-done), kind=kOutput, calls=%fused_computation.11 | convolution fusion | flops 1616115328 | bytes 9718784 | tf_op jit(solution)/shard_map/dot_general | solution.py:31
  199.4 102.1 %psum.14 = f32[1,2048]{1,0:T(1,128)} all-reduce(f32[1,2048]{1,0:T(1,128)S(1)} %bitcast.52), channel_id=1, replica_groups=mesh['rep'=16,'fsdp'=32] {'fsdp'}, use_global_device_ids=true, to_apply=%region_3.0 | all-reduce | flops 2048 | bytes 16384 | tf_op jit(solution)/shard_map/psum | solution.py:37
  301.6 3.9 %fusion.17 = bf16[1,384,2048]{2,1,0:T(8,128)(2,1)} fusion(bf16[1,384,2048]{2,1,0:T(8,128)(2,1)S(1)} %copy-done.1, f32[384,2048]{1,0:T(8,128)} %get-tuple-element.9, f32[384]{0:T(512)S(1)} %broadcast_multiply_fusion, f32[2048]{0:T(1024)S(1)} %bitcast.51, f32[384]{0:T(512)S(1)} %add_rsqrt_fusion), kind=kLoop, calls=%fused_computation.19 | loop fusion | flops 5505024 | bytes 6302720 | tf_op jit(solution)/shard_map/broadcast_in_dim | solution.py:41
  305.4 0.0 reduce-scatter.2.cloned.1.call-done
  (2 shorter events, 0.0 us)
Async XLA Ops:
  8.0 4.1 %copy-start = (bf16[1,384,1024]{2,1,0:T(8,128)(2,1)S(1)}, bf16[1,384,1024]{2,1,0:T(8,128)(2,1)}, u32[]{:S(2)}) copy-start(bf16[1,384,1024]{2,1,0:T(8,128)(2,1)} %param.11) | copy-start | bytes 2359300
  8.0 183.7 %all-reduce.2.cloned.1.call-start = ((), (), s32[]{:S(2)}) async-start(), calls=%async_computation.2 | async-start | bytes 131072 | tf_op jit(solution)/shard_map/psum | solution.py:54
  9.7 183.6 %all-gather.3.cloned.1.call-start = ((), (), s32[]{:S(2)}) async-start(), calls=%async_computation.3 | async-start | bytes 4325376 | tf_op jit(solution)/shard_map/all_gather | solution.py:33
  10.3 295.2 %reduce-scatter.2.cloned.1.call-start = ((), (), s32[]{:S(2)}) async-start(), calls=%async_computation.1 | async-start | bytes 4325376 | tf_op jit(solution)/shard_map/reduce_scatter | solution.py:23
  17.9 173.8 %copy-start.2 = (f32[16,2048]{1,0:T(8,128)S(1)}, f32[16,2048]{1,0:T(8,128)}, u32[]{:S(2)}) copy-start(f32[16,2048]{1,0:T(8,128)} %param.14) | copy-start | bytes 393220
  17.9 173.8 %copy-start.3 = (f32[16,2048]{1,0:T(8,128)S(1)}, f32[16,2048]{1,0:T(8,128)}, u32[]{:S(2)}) copy-start(f32[16,2048]{1,0:T(8,128)} %param.13) | copy-start | bytes 393220
  17.9 175.4 %copy-start.1 = (bf16[1,384,2048]{2,1,0:T(8,128)(2,1)S(1)}, bf16[1,384,2048]{2,1,0:T(8,128)(2,1)}, u32[]{:S(2)}) copy-start(bf16[1,384,2048]{2,1,0:T(8,128)(2,1)} %param.8) | copy-start | bytes 4718596
  17.9 175.4 %copy-start.4 = (f32[1,2048]{1,0:T(1,128)S(1)}, f32[1,2048]{1,0:T(1,128)}, u32[]{:S(2)}) copy-start(f32[1,2048]{1,0:T(1,128)} %param.9) | copy-start | bytes 24580
Sparse Core Ops, SparseCore 0:
  12.6 179.0 all-reduce.1
Sparse Core Ops, SparseCore 1:
  13.3 101.4 all-gather.2
  119.7 132.9 reduce-scatter.1
where the time goes:
time: 318 us; the launch traced here: 313 us
  waiting for transfers between devices  173 us (54%)
  blocking collectives  102 us (32%)
  between operations  16.4 us (5%)
  matrix products  11.9 us (4%)
  other arithmetic  8.84 us (3%)
    psum x1, waiting for transfers between devices, outer_step(): lax.psum(outer_delta[0].astype(jnp.bfloat16), 'rep').astype(jnp.float32)  173 us
    psum x1, blocking collectives, inner_step(): grad_gain = lax.psum(jnp.sum(normed_grad * unit, axis=0), 'fsdp')  102 us
  transfers between devices with their start and end apart: 3, of which 1 were waited for; matrix products, arithmetic and copies ran while one was open for 6% of the time, Pallas kernels for 0%

commit v1 on v0

v1 whole, which is shorter than its diff:
```python
import functools

import jax
import jax.numpy as jnp
from jax import lax
from jax.experimental import pallas as pl
from jax.experimental.pallas import tpu as pltpu
from jax.sharding import PartitionSpec as P

ROUNDS = 64
EPSILON = 1e-05
NESTEROV_MU = 0.9
OUTER_RATE = 0.7
MESH = pl.DeviceIdType.MESH
F32, BF16 = jnp.float32, jnp.bfloat16
LANES = 128


def kernel(
    sizes,
    resid_hbm,
    gain_hbm,
    w_hbm,
    kv_hbm,
    delta_hbm,
    mom_hbm,
    par_hbm,
    sync_ref,
    gkv_out,
    ggain_out,
    gin_hbm,
    npar_out,
    nmom_out,
    x,
    gain,
    wbuf,
    kv,
    kv_sib,
    nt,
    nt_sib,
    pb,
    ybuf,
    yb,
    zbuf,
    scale,
    acc,
    gb,
    obuf,
    gs,
    gsib,
    gy,
    gz,
    delta,
    mom,
    par,
    dl,
    dx,
    dz,
    dt,
    sem_in,
    sem_out,
    az_s,
    az_r,
    ay_s,
    ay_r,
    as_s,
    as_r,
    nt_s,
    nt_r,
    ry_s,
    ry_r,
    rz_s,
    rz_r,
    ox_s,
    ox_r,
    og_s,
    og_r,
    gg_s,
    gg_r,
):
    tok, feat, kvw, outer = sizes
    rows = w_hbm.shape[0]
    half = rows // 2
    pair = 2 * rows
    chunks = feat // pair
    f = lax.axis_index("fsdp")
    c = lax.rem(f, 2)
    y = lax.rem(lax.div(f, 2), 4)
    h = lax.div(f, 8)
    rep = lax.axis_index("rep")
    xx = lax.rem(rep, 4)
    zl = lax.div(rep, 4)

    def mod4(v):
        return lax.rem(v + 8, 4)

    def inside(hh, yy, cc):
        return {"fsdp": (hh * 4 + yy) * 2 + cc}

    sib = inside(h, y, 1 - c)
    y_peer = {s: inside(h, mod4(y + s), c) for s in (1, -1, 2)}
    h_peer = {s: inside(mod4(h + s), y, c) for s in (1, -1, 2)}
    x_peer = {s: {"rep": zl * 4 + mod4(xx + s)} for s in (1, 2, 3)}
    l_peer = {s: {"rep": mod4(zl + s) * 4 + xx} for s in (1, 2, 3)}

    barrier = pltpu.get_barrier_semaphore()
    peers = [sib] + list(y_peer.values()) + list(h_peer.values())
    if outer:
        peers += list(x_peer.values()) + list(l_peer.values())
    for peer in peers:
        pl.semaphore_signal(barrier, inc=1, device_id=peer, device_id_type=MESH)

    def blk(p, yy, cc, part=None):
        start = ((p * 4 + yy) * 2 + cc) * rows
        if part is None:
            return wbuf.at[pl.ds(pl.multiple_of(start, rows), rows), :]
        return wbuf.at[pl.ds(pl.multiple_of(start + part * half, half), half), :]

    own_copies = [
        (resid_hbm, x),
        (kv_hbm, kv),
        (gain_hbm, gain),
        (w_hbm, blk(h, y, c)),
        (delta_hbm, delta),
        (mom_hbm, mom),
        (par_hbm, par),
    ]
    loads = [pltpu.make_async_copy(a, b, sem_in.at[i]) for i, (a, b) in enumerate(own_copies)]
    for load in loads:
        load.start()

    pending = []

    def send(src, dst, ssem, rsem, peer):
        copy = pltpu.make_async_remote_copy(
            src_ref=src, dst_ref=dst, send_sem=ssem, recv_sem=rsem, device_id=peer, device_id_type=MESH
        )
        copy.start()
        pending.append(copy)

    def landed(dst, ssem, rsem, peer):
        pltpu.make_async_remote_copy(
            src_ref=dst, dst_ref=dst, send_sem=ssem, recv_sem=rsem, device_id=peer, device_id_type=MESH
        ).wait_recv()

    pl.semaphore_wait(barrier, len(peers))

    PART = (0, 1, 1, 0, 0, 1)
    WAY = (1, -1, 1, -1, 1, -1)

    def az_send(k):
        if k < 4:
            src = w_hbm.at[pl.ds(PART[k] * half, half), :]
            dst = blk(h, y, c, PART[k])
        else:
            src = dst = blk(mod4(h - WAY[k]), y, c, PART[k])
        send(src, dst, az_s.at[k], az_r.at[k], h_peer[WAY[k]])

    def az_wait(k):
        p = mod4(h - WAY[k] * (1 if k < 4 else 2))
        landed(blk(p, y, c, PART[k]), az_s.at[k], az_r.at[k], h_peer[WAY[k]])

    def ay_send(d, k):
        p = mod4(h + d)
        if k < 4:
            dst = blk(p, y, c, PART[k])
            src = w_hbm.at[pl.ds(PART[k] * half, half), :] if d == 0 else dst
        else:
            src = dst = blk(p, mod4(y - WAY[k]), c, PART[k])
        send(src, dst, ay_s.at[d, k], ay_r.at[d, k], y_peer[WAY[k]])

    def ay_wait(d, k):
        yy = mod4(y - WAY[k] * (1 if k < 4 else 2))
        landed(blk(mod4(h + d), yy, c, PART[k]), ay_s.at[d, k], ay_r.at[d, k], y_peer[WAY[k]])

    def as_send(d, r):
        b = blk(mod4(h + d), mod4(y + r), c)
        src = w_hbm if (d, r) == (0, 0) else b
        send(src, b, as_s.at[d, r], as_r.at[d, r], sib)

    def as_wait(d, r):
        landed(blk(mod4(h + d), mod4(y + r), 1 - c), as_s.at[d, r], as_r.at[d, r], sib)

    for k in (0, 1, 2, 3):
        az_send(k)
    for k in (0, 1, 2, 3):
        ay_send(0, k)
    loads[1].wait()
    send(kv, kv_sib, nt_s.at[4], nt_r.at[4], sib)
    as_send(0, 0)

    loads[0].wait()
    loads[2].wait()

    @pl.loop(0, tok // 32)
    def _(i):
        at = pl.ds(pl.multiple_of(i * 32, 32), 32)
        v = x[at, :].astype(F32)
        mean = jnp.mean(v * v, axis=-1, keepdims=True)
        scale[at, :] = jnp.broadcast_to(lax.rsqrt(mean + EPSILON), (32, LANES))

    def norm(d):
        p = mod4(h + d)

        @pl.loop(0, 4)
        def _(yy):
            lanes = pl.ds(pl.multiple_of((p * 4 + yy) * pair, pair), pair)
            unit = x[:, lanes].astype(F32) * scale[...]
            t = (unit * gain[0:1, lanes]).astype(BF16).T
            at = pl.ds(pl.multiple_of(yy * rows, rows), rows)
            nt[0, d, at, :] = t[:rows]
            nt[1, d, at, :] = t[rows:]

        send(nt.at[1 - c, d], nt_sib.at[d], nt_s.at[d], nt_r.at[d], sib)

    def partial(d):
        landed(nt_sib.at[d], nt_s.at[d], nt_r.at[d], sib)
        step = min(256, kvw)

        @pl.loop(0, kvw // step)
        def _(i):
            at = pl.ds(pl.multiple_of(i * step, step), step)
            t = jnp.dot(nt[c, d], kv[:, at], preferred_element_type=F32)
            t = t + jnp.dot(nt_sib[d], kv_sib[:, at], preferred_element_type=F32)
            pb[d, :, at] = t.astype(BF16)

        for k in (0, 1, 2, 3):
            ry_send(d, k)

    def piece(d, yy, part):
        return pl.ds(pl.multiple_of(mod4(yy) * rows + part * half, half), half)

    def ry_send(d, k):
        dest = y + (2 * WAY[k] if k < 2 else WAY[k])
        send(pb.at[d, piece(d, dest, PART[k]), :], ybuf.at[d, k], ry_s.at[d, k], ry_r.at[d, k], y_peer[WAY[k]])

    def ry_wait(d, k):
        landed(ybuf.at[d, k], ry_s.at[d, k], ry_r.at[d, k], y_peer[WAY[k]])

    def ry_mid(d):
        for k in (0, 1):
            ry_wait(d, k)
            at = piece(d, y + WAY[k], PART[k])
            pb[d, at, :] = (pb[d, at, :].astype(F32) + ybuf[d, k].astype(F32)).astype(BF16)
            ry_send(d, k + 4)

    def ry_end(d):
        for part, ks in ((0, (3, 4)), (1, (2, 5))):
            for k in ks:
                ry_wait(d, k)
            t = pb[d, piece(d, y, part), :].astype(F32)
            for k in ks:
                t = t + ybuf[d, k].astype(F32)
            yb[d, part] = t.astype(BF16)

    def rz_send(k):
        d = 2 if k < 2 else WAY[k] % 4
        send(yb.at[d, PART[k]], zbuf.at[k], rz_s.at[k], rz_r.at[k], h_peer[WAY[k]])

    def rz_wait(k):
        landed(zbuf.at[k], rz_s.at[k], rz_r.at[k], h_peer[WAY[k]])

    def rz_mid(k):
        rz_wait(k)
        d, part = WAY[k] % 4, PART[k]
        yb[d, part] = (yb[d, part].astype(F32) + zbuf[k].astype(F32)).astype(BF16)
        rz_send(k + 4)

    def rz_end():
        for part, ks in ((0, (3, 4)), (1, (2, 5))):
            for k in ks:
                rz_wait(k)
            t = yb[0, part].astype(F32)
            for k in ks:
                t = t + zbuf[k].astype(F32)
            gkv_out[part * half : (part + 1) * half, :] = t.astype(BF16)

    def chunk(d, r):
        j = mod4(h + d) * 4 + mod4(y + r)
        lanes = pl.ds(pl.multiple_of(j * pair, pair), pair)
        ng = lax.dot_general(kv[...], wbuf[lanes, :], (((1,), (1,)), ((), ())), preferred_element_type=F32)
        unit = x[:, lanes].astype(F32) * scale[...]
        gs[pl.ds(j, 1), :] = jnp.sum(ng * unit, axis=0, keepdims=True)
        g = ng * gain[0:1, lanes]
        acc[...] += g * unit
        gb[:, lanes] = g

    def plane(d):
        for r in (0, 3, 1, 2):
            as_wait(d, r)
            chunk(d, r)

    def outer_first():
        loads[4].wait()
        width = feat // 4
        for i in range(4):
            dl[i] = delta[:, i * width : (i + 1) * width].astype(BF16)
        for s in (1, 2, 3):
            send(dl.at[mod4(xx + s)], dx.at[s], ox_s.at[s], ox_r.at[s], x_peer[s])

    def outer_second():
        t = dl[xx].astype(F32)
        for s in (1, 2, 3):
            landed(dx.at[s], ox_s.at[s], ox_r.at[s], x_peer[s])
            t = t + dx[s].astype(F32)
        dz[zl] = t.astype(BF16)
        for s in (1, 2, 3):
            send(dz.at[zl], dz.at[zl], og_s.at[0, s], og_r.at[0, s], l_peer[s])

    def outer_third():
        for s in (1, 2, 3):
            landed(dz.at[mod4(zl - s)], og_s.at[0, s], og_r.at[0, s], l_peer[s])
        t = dz[0].astype(F32) + dz[1].astype(F32) + dz[2].astype(F32) + dz[3].astype(F32)
        dt[xx] = t.astype(BF16)
        for s in (1, 2, 3):
            send(dt.at[xx], dt.at[xx], og_s.at[1, s], og_r.at[1, s], x_peer[s])

    def outer_last():
        for s in (1, 2, 3):
            landed(dt.at[mod4(xx - s)], og_s.at[1, s], og_r.at[1, s], x_peer[s])
        loads[5].wait()
        loads[6].wait()
        width = feat // 4
        phase = jnp.full((1, LANES), sync_ref[0].astype(F32)) / ROUNDS
        rate = (OUTER_RATE * (1.0 + jnp.cos(jnp.pi * phase)) / 2.0)[0:1, 0:1]
        for i in range(4):
            at = slice(i * width, (i + 1) * width)
            mean = dt[i].astype(F32) * (1.0 / 16)
            fresh = NESTEROV_MU * mom[:, at] + mean
            nmom_out[:, at] = fresh
            npar_out[:, at] = par[:, at] - rate * (mean + NESTEROV_MU * fresh)

    acc[...] = jnp.zeros_like(acc)
    norm(2)
    norm(1)
    landed(kv_sib, nt_s.at[4], nt_r.at[4], sib)
    partial(2)
    for k in (0, 1):
        ay_wait(0, k)
        ay_send(0, k + 4)
    norm(3)
    partial(1)
    norm(0)
    partial(3)
    partial(0)
    if outer:
        outer_first()
    ry_mid(2)
    for k in (2, 3):
        ay_wait(0, k)
    as_send(0, 3)
    as_send(0, 1)
    loads[3].wait()
    az_wait(0)
    az_send(4)
    ay_send(3, 0)
    ay_send(3, 3)
    az_wait(1)
    az_send(5)
    ay_send(1, 1)
    ay_send(1, 2)
    ry_mid(1)
    ry_end(2)
    rz_send(0)
    rz_send(1)
    if outer:
        outer_second()
    ry_mid(3)
    ay_wait(0, 4)
    ay_wait(0, 5)
    as_send(0, 2)
    ry_mid(0)
    plane(0)
    az_wait(2)
    ay_send(3, 1)
    ay_send(3, 2)
    az_wait(3)
    ay_send(1, 0)
    ay_send(1, 3)
    as_send(3, 0)
    as_send(1, 0)
    ry_end(1)
    rz_send(2)
    ry_end(3)
    rz_send(3)
    if outer:
        outer_third()
    rz_mid(0)
    rz_mid(1)
    ry_end(0)
    az_wait(4)
    ay_send(2, 0)
    ay_send(2, 3)
    az_wait(5)
    ay_send(2, 1)
    ay_send(2, 2)
    as_send(2, 0)
    for k in (0, 1):
        ay_wait(3, k)
        ay_send(3, k + 4)
    for k in (0, 1):
        ay_wait(1, k)
        ay_send(1, k + 4)
    if outer:
        outer_last()
    for d in (3, 1):
        for k in (2, 3):
            ay_wait(d, k)
        as_send(d, 3)
        as_send(d, 1)
    for k in (0, 1):
        ay_wait(2, k)
        ay_send(2, k + 4)
    for d in (3, 1):
        for k in (4, 5):
            ay_wait(d, k)
        as_send(d, 2)
        plane(d)
    for k in (2, 3):
        ay_wait(2, k)
    as_send(2, 3)
    as_send(2, 1)
    for k in (4, 5):
        ay_wait(2, k)
    as_send(2, 2)
    plane(2)

    send(gs, gsib, gg_s.at[0], gg_r.at[0], sib)
    inner = jnp.sum(acc[...], axis=-1, keepdims=True) * (1.0 / feat)
    acc[...] = jnp.broadcast_to(inner, acc.shape)
    landed(gsib, gg_s.at[0], gg_r.at[0], sib)
    gy[y] = gs[...] + gsib[...]
    for s in (1, -1, 2):
        send(gy.at[y], gy.at[y], gg_s.at[2 + s], gg_r.at[2 + s], y_peer[s])

    outs = []
    block = min(64, tok)

    def final(i):
        at = slice(i * block, (i + 1) * block)
        sc, inn = scale[at, :], acc[at, :]
        for j in range(chunks):
            lanes = slice(j * pair, (j + 1) * pair)
            unit = x[at, lanes].astype(F32) * sc
            obuf[at, lanes] = (sc * (gb[at, lanes] - unit * inn)).astype(BF16)
        out = pltpu.make_async_copy(obuf.at[at, :], gin_hbm.at[at, :], sem_out.at[i])
        out.start()
        outs.append(out)

    n_final = tok // block
    for i in range(n_final):
        if i == n_final // 2:
            for s in (1, -1, 2):
                landed(gy.at[mod4(y - s)], gg_s.at[2 + s], gg_r.at[2 + s], y_peer[s])
            gz[h] = gy[0] + gy[1] + gy[2] + gy[3]
            for s in (1, -1, 2):
                send(gz.at[h], gz.at[h], gg_s.at[6 + s], gg_r.at[6 + s], h_peer[s])
        final(i)

    rz_end()
    for s in (1, -1, 2):
        landed(gz.at[mod4(h - s)], gg_s.at[6 + s], gg_r.at[6 + s], h_peer[s])
    total = gz[0] + gz[1] + gz[2] + gz[3]
    for j in range(chunks):
        ggain_out[0:1, j * pair : (j + 1) * pair] = total[j : j + 1, :]
    for copy in pending:
        copy.wait_send()
    for out in outs:
        out.wait()


def local(residual_in, norm_gain, kv_weight, kv_grad, outer_delta, outer_momentum, global_params, sync_index, outer=True):
    tok, feat = residual_in.shape[1:]
    rows, kvw = kv_weight.shape[1:]
    frag = outer_delta.shape[1]
    half, pair = rows // 2, 2 * rows
    chunks = feat // pair
    any_space = pl.BlockSpec(memory_space=pl.ANY)
    vmem = pl.BlockSpec(memory_space=pltpu.VMEM)
    dma = pltpu.SemaphoreType.DMA
    width = feat // 4
    grad_kv, grad_gain, grad_input, new_params, new_momentum = pl.pallas_call(
        functools.partial(kernel, (tok, feat, kvw, outer)),
        out_shape=(
            jax.ShapeDtypeStruct((rows, kvw), BF16),
            jax.ShapeDtypeStruct((1, feat), F32),
            jax.ShapeDtypeStruct((tok, feat), BF16),
            jax.ShapeDtypeStruct((frag, feat), F32),
            jax.ShapeDtypeStruct((frag, feat), F32),
        ),
        in_specs=[any_space] * 7 + [pl.BlockSpec(memory_space=pltpu.SMEM)],
        out_specs=(vmem, vmem, any_space, vmem, vmem),
        scratch_shapes=[
            pltpu.VMEM((tok, feat), BF16),
            pltpu.VMEM((1, feat), F32),
            pltpu.VMEM((feat, kvw), BF16),
            pltpu.VMEM((tok, kvw), BF16),
            pltpu.VMEM((tok, kvw), BF16),
            pltpu.VMEM((2, 4, 4 * rows, tok), BF16),
            pltpu.VMEM((4, 4 * rows, tok), BF16),
            pltpu.VMEM((4, 4 * rows, kvw), BF16),
            pltpu.VMEM((4, 6, half, kvw), BF16),
            pltpu.VMEM((4, 2, half, kvw), BF16),
            pltpu.VMEM((6, half, kvw), BF16),
            pltpu.VMEM((tok, LANES), F32),
            pltpu.VMEM((tok, LANES), F32),
            pltpu.VMEM((tok, feat), F32),
            pltpu.VMEM((tok, feat), BF16),
            pltpu.VMEM((chunks, pair), F32),
            pltpu.VMEM((chunks, pair), F32),
            pltpu.VMEM((4, chunks, pair), F32),
            pltpu.VMEM((4, chunks, pair), F32),
            pltpu.VMEM((frag, feat), F32),
            pltpu.VMEM((frag, feat), F32),
            pltpu.VMEM((frag, feat), F32),
            pltpu.VMEM((4, frag, width), BF16),
            pltpu.VMEM((4, frag, width), BF16),
            pltpu.VMEM((4, frag, width), BF16),
            pltpu.VMEM((4, frag, width), BF16),
            dma((7,)),
            dma((tok // min(64, tok),)),
            dma((6,)),
            dma((6,)),
            dma((4, 6)),
            dma((4, 6)),
            dma((4, 4)),
            dma((4, 4)),
            dma((5,)),
            dma((5,)),
            dma((4, 6)),
            dma((4, 6)),
            dma((6,)),
            dma((6,)),
            dma((4,)),
            dma((4,)),
            dma((2, 4)),
            dma((2, 4)),
            dma((9,)),
            dma((9,)),
        ],
        compiler_params=pltpu.CompilerParams(
            collective_id=0, has_side_effects=True, vmem_limit_bytes=56 * 1024 * 1024
        ),
    )(
        residual_in[0],
        norm_gain,
        kv_weight[0],
        kv_grad[0],
        outer_delta[0],
        outer_momentum,
        global_params,
        sync_index,
    )
    return (grad_kv[None], grad_gain, grad_input[None], new_params, new_momentum)


def solution(mesh):
    placed = (
        P("rep", "fsdp", None),
        P("rep", None),
        P("rep", "fsdp", None),
        P("rep", "fsdp", None),
        P("rep", "fsdp", None),
        P("fsdp", None),
        P("fsdp", None),
        P(),
    )
    return jax.shard_map(
        local,
        mesh=mesh,
        in_specs=placed,
        out_specs=(
            P("rep", "fsdp", None),
            P("rep", None),
            P("rep", "fsdp", None),
            P("fsdp", None),
            P("fsdp", None),
        ),
        check_vma=False,
    )
```

time: 318 us -> 83.6 us (0.26); the launches traced: 313 us -> 82.1 us
  waiting for transfers between devices: 173 us -> 0 us
  blocking collectives: 102 us -> 0 us
  Pallas kernels: 0 us -> 73.8 us
  between operations: 16.4 us -> 1.29 us
  matrix products: 11.9 us -> 0 us
  other arithmetic: 8.84 us -> 0 us
  local copies, waits for them, and re-layouts: 0.02 us -> 6.95 us
    psum x1 -> x0, waiting for transfers between devices: 173 us -> none  [outer_step(): lax.psum(outer_delta[0].astype(jnp.bfloat16), 'rep').astype(jnp.float32)]
    psum x1 -> x0, blocking collectives: 102 us -> none  [inner_step(): grad_gain = lax.psum(jnp.sum(normed_grad * unit, axis=0), 'fsdp')]
    pallas_call x0 -> x1, Pallas kernels: none -> 73.8 us  [local(): pl.pallas_call(functools.partial(kernel, (tok, feat, kvw, outer)), out_sh...]
    dot_general x2 -> x0, matrix products: 11.9 us -> none  [the longest x1 6.14 us: inner_step(): lax.dot_general(grads_here, lax.all_gather(kv_weight[0], 'fsdp', axis=0,...]
    unnamed x10 -> x9, local copies, waits for them, and re-layouts: 0.02 us -> 6.95 us
    broadcast_in_dim x1 -> x0, other arithmetic: 3.86 us -> none  [inner_step(): return (grad_kv[None], grad_gain[None], grad_input[None])]
  transfers between devices with their start and end apart: 3 -> 0, of which waited for: 1 -> 0; matrix products, arithmetic and copies ran while one was open for 6% -> 0% of each run, Pallas kernels for 0% -> 0%
where the time goes in v1:
time: 83.6 us; the launch traced here: 82.1 us
  Pallas kernels  73.8 us (88%)
  local copies, waits for them, and re-layouts  6.95 us (8%)
  between operations  1.29 us (2%)
    pallas_call x1, Pallas kernels, local(): pl.pallas_call(functools.partial(kernel, (tok, feat, kvw, outer)), out_sh...  73.8 us
    unnamed x9, local copies, waits for them, and re-layouts  6.95 us

profile of v1, /device:TPU:1, one launch (start us, length us, event | category | flops | bytes accessed | tf_op | source)
XLA Modules:
  0.0 82.1 jit_solution(10480085459549175021)
XLA Ops:
  1.3 73.8 %shard_map.119 = (bf16[64,1024]{1,0:T(8,128)(2,1)}, f32[1,2048]{1,0:T(1,128)}, bf16[384,2048]{1,0:T(8,128)(2,1)}, f32[16,2048]{1,0:T(8,128)}, f32[16,2048]{1,0:T(8,128)}) custom-call(bf16[384,2048]{1,0:T(8,128)(2,1)} %bitcast.6, f32[1,2048]{1,0:T(1,128)} %gain_hbm.1, bf16[64,1024]{1,0:T(8,128)(2,1)} %bitcast.9, bf16[384,1024]{1,0:T(8,128)(2,1)} %bitcast.8, ...), custom_call_target="tpu_custom_call" | custom-call | tf_op jit(solution)/shard_map/pallas_call | solution.py:482
  75.1 1.6 %copy.19 = bf16[1,64,1024]{2,1,0:T(8,128)(2,1)} copy(bf16[1,64,1024]{2,1,0:T(8,128)(2,1)} %bitcast.11) | data formatting | bytes 262144
  76.7 1.3 %copy.20 = f32[1,2048]{1,0:T(1,128)} copy(f32[1,2048]{1,0:T(1,128)} %get-tuple-element.21) | data formatting | bytes 16384
  78.0 0.0 copy-start.1
  78.0 0.0 copy-start
  78.0 2.8 %copy.21 = bf16[1,384,2048]{2,1,0:T(8,128)(2,1)} copy(bf16[1,384,2048]{2,1,0:T(8,128)(2,1)} %bitcast.7) | data formatting | bytes 3145728
  80.8 0.0 copy-done.1
  80.8 0.7 copy.22
  81.4 0.0 copy-done
  81.4 0.7 copy.23
Async XLA Ops:
  78.0 2.8 %copy-start.1 = (f32[16,2048]{1,0:T(8,128)S(1)}, f32[16,2048]{1,0:T(8,128)}, u32[]{:S(2)}) copy-start(f32[16,2048]{1,0:T(8,128)} %get-tuple-element.23) | copy-start | bytes 393220
  78.0 3.4 %copy-start = (f32[16,2048]{1,0:T(8,128)S(1)}, f32[16,2048]{1,0:T(8,128)}, u32[]{:S(2)}) copy-start(f32[16,2048]{1,0:T(8,128)} %get-tuple-element.24) | copy-start | bytes 393220

commit v2 on v1

--- a/solution.py
+++ b/solution.py
@@ -14,6 +14,97 @@
 MESH = pl.DeviceIdType.MESH
 F32, BF16 = jnp.float32, jnp.bfloat16
 LANES = 128
+
+
+ORDER = (
+    ("norm", 2),
+    ("norm", 1),
+    ("norm", 3),
+    ("ay_fwd", 0, 4),
+    ("ay_fwd", 0, 5),
+    ("over", 0, 1),
+    ("over", 0, 3),
+    ("kv_here",),
+    ("partial", 2),
+    ("partial", 1),
+    ("partial", 3),
+    ("outer_first",),
+    ("over", 0, 2),
+    ("mul", 0, 0),
+    ("mul", 0, 1),
+    ("mul", 0, 3),
+    ("mul", 0, 2),
+    ("outer_second",),
+    ("az_fwd", 4),
+    ("az_fwd", 5),
+    ("ry_mid", 2, 0),
+    ("ry_mid", 2, 1),
+    ("over", 1, 0),
+    ("outer_third",),
+    ("over", 3, 0),
+    ("ry_mid", 1, 0),
+    ("ry_mid", 1, 1),
+    ("ry_mid", 3, 0),
+    ("ry_mid", 3, 1),
+    ("ay_first", 3, 0),
+    ("ay_first", 1, 1),
+    ("outer_last",),
+    ("ry_end", 2, 1),
+    ("ry_end", 2, 0),
+    ("ay_first", 1, 0),
+    ("rz_send", 0),
+    ("rz_send", 1),
+    ("mul", 3, 0),
+    ("ry_end", 1, 0),
+    ("ry_end", 1, 1),
+    ("rz_send", 2),
+    ("ay_first", 3, 1),
+    ("over", 2, 0),
+    ("ry_end", 3, 0),
+    ("ry_end", 3, 1),
+    ("ay_fwd", 1, 5),
+    ("ay_fwd", 3, 4),
+    ("norm", 0),
+    ("ay_fwd", 1, 4),
+    ("over", 1, 1),
+    ("over", 1, 3),
+    ("ay_first", 2, 0),
+    ("ay_first", 2, 1),
+    ("rz_send", 3),
+    ("mul", 1, 0),
+    ("mul", 2, 0),
+    ("over", 3, 3),
+    ("ay_fwd", 3, 5),
+    ("over", 3, 1),
+    ("mul", 1, 1),
+    ("partial", 0),
+    ("rz_mid", 1),
+    ("mul", 1, 3),
+    ("mul", 3, 1),
+    ("mul", 3, 3),
+    ("rz_mid", 0),
+    ("ay_fwd", 2, 5),
+    ("over", 2, 1),
+    ("over", 1, 2),
+    ("ay_fwd", 2, 4),
+    ("over", 2, 3),
+    ("over", 3, 2),
+    ("mul", 2, 1),
+    ("mul", 1, 2),
+    ("mul", 2, 3),
+    ("ry_mid", 0, 0),
+    ("ry_mid", 0, 1),
+    ("mul", 3, 2),
+    ("over", 2, 2),
+    ("mul", 2, 2),
+    ("ry_end", 0, 0),
+    ("ry_end", 0, 1),
+)
+LATE = (
+    ("rz_end", 0),
+    ("rz_end", 1),
+    ("gain_send",),
+)
 
 
 def kernel(
@@ -46,10 +137,8 @@
     acc,
     gb,
     obuf,
-    gs,
-    gsib,
-    gy,
-    gz,
+    gfold,
+    gall,
     delta,
     mom,
     par,
@@ -104,7 +193,9 @@
     l_peer = {s: {"rep": mod4(zl + s) * 4 + xx} for s in (1, 2, 3)}
 
     barrier = pltpu.get_barrier_semaphore()
-    peers = [sib] + list(y_peer.values()) + list(h_peer.values())
+    size = 2 * chunks
+    f_peer = {s: {"fsdp": lax.rem(f + s, size)} for s in range(1, size)}
+    peers = list(f_peer.values())
     if outer:
         peers += list(x_peer.values()) + list(l_peer.values())
     for peer in peers:
@@ -126,8 +217,8 @@
         (par_hbm, par),
     ]
     loads = [pltpu.make_async_copy(a, b, sem_in.at[i]) for i, (a, b) in enumerate(own_copies)]
-    for load in loads:
-        load.start()
+    for i in (3, 1, 0, 2, 4, 5, 6):
+        loads[i].start()
 
     pending = []
 
@@ -143,15 +234,22 @@
             src_ref=dst, dst_ref=dst, send_sem=ssem, recv_sem=rsem, device_id=peer, device_id_type=MESH
         ).wait_recv()
 
+    loads[3].wait()
     pl.semaphore_wait(barrier, len(peers))
+
+    seen = set()
+
+    def need(wait, *key):
+        if (wait, key) not in seen:
+            seen.add((wait, key))
+            wait(*key)
 
     PART = (0, 1, 1, 0, 0, 1)
     WAY = (1, -1, 1, -1, 1, -1)
 
     def az_send(k):
         if k < 4:
-            src = w_hbm.at[pl.ds(PART[k] * half, half), :]
-            dst = blk(h, y, c, PART[k])
+            src = dst = blk(h, y, c, PART[k])
         else:
             src = dst = blk(mod4(h - WAY[k]), y, c, PART[k])
         send(src, dst, az_s.at[k], az_r.at[k], h_peer[WAY[k]])
@@ -163,8 +261,7 @@
     def ay_send(d, k):
         p = mod4(h + d)
         if k < 4:
-            dst = blk(p, y, c, PART[k])
-            src = w_hbm.at[pl.ds(PART[k] * half, half), :] if d == 0 else dst
+            src = dst = blk(p, y, c, PART[k])
         else:
             src = dst = blk(p, mod4(y - WAY[k]), c, PART[k])
         send(src, dst, ay_s.at[d, k], ay_r.at[d, k], y_peer[WAY[k]])
@@ -175,8 +272,7 @@
 
     def as_send(d, r):
         b = blk(mod4(h + d), mod4(y + r), c)
-        src = w_hbm if (d, r) == (0, 0) else b
-        send(src, b, as_s.at[d, r], as_r.at[d, r], sib)
+        send(b, b, as_s.at[d, r], as_r.at[d, r], sib)
 
     def as_wait(d, r):
         landed(blk(mod4(h + d), mod4(y + r), 1 - c), as_s.at[d, r], as_r.at[d, r], sib)
@@ -237,21 +333,20 @@
     def ry_wait(d, k):
         landed(ybuf.at[d, k], ry_s.at[d, k], ry_r.at[d, k], y_peer[WAY[k]])
 
-    def ry_mid(d):
-        for k in (0, 1):
-            ry_wait(d, k)
-            at = piece(d, y + WAY[k], PART[k])
-            pb[d, at, :] = (pb[d, at, :].astype(F32) + ybuf[d, k].astype(F32)).astype(BF16)
-            ry_send(d, k + 4)
-
-    def ry_end(d):
-        for part, ks in ((0, (3, 4)), (1, (2, 5))):
-            for k in ks:
-                ry_wait(d, k)
-            t = pb[d, piece(d, y, part), :].astype(F32)
-            for k in ks:
-                t = t + ybuf[d, k].astype(F32)
-            yb[d, part] = t.astype(BF16)
+    ENDS = ((3, 4), (2, 5))
+
+    def ry_mid(d, k):
+        need(ry_wait, d, k)
+        at = piece(d, y + WAY[k], PART[k])
+        pb[d, at, :] = (pb[d, at, :].astype(F32) + ybuf[d, k].astype(F32)).astype(BF16)
+        ry_send(d, k + 4)
+
+    def ry_end(d, part):
+        t = pb[d, piece(d, y, part), :].astype(F32)
+        for k in ENDS[part]:
+            need(ry_wait, d, k)
+            t = t + ybuf[d, k].astype(F32)
+        yb[d, part] = t.astype(BF16)
 
     def rz_send(k):
         d = 2 if k < 2 else WAY[k] % 4
@@ -261,34 +356,43 @@
         landed(zbuf.at[k], rz_s.at[k], rz_r.at[k], h_peer[WAY[k]])
 
     def rz_mid(k):
-        rz_wait(k)
+        need(rz_wait, k)
         d, part = WAY[k] % 4, PART[k]
         yb[d, part] = (yb[d, part].astype(F32) + zbuf[k].astype(F32)).astype(BF16)
         rz_send(k + 4)
 
-    def rz_end():
-        for part, ks in ((0, (3, 4)), (1, (2, 5))):
-            for k in ks:
-                rz_wait(k)
-            t = yb[0, part].astype(F32)
-            for k in ks:
-                t = t + zbuf[k].astype(F32)
-            gkv_out[part * half : (part + 1) * half, :] = t.astype(BF16)
+    def rz_end(part):
+        t = yb[0, part].astype(F32)
+        for k in ENDS[part]:
+            need(rz_wait, k)
+            t = t + zbuf[k].astype(F32)
+        gkv_out[part * half : (part + 1) * half, :] = t.astype(BF16)
+        t = t * blk(h, y, c, part)[...].astype(F32)
+        fold = t[:, :LANES]
+        for i in range(1, kvw // LANES):
+            fold = fold + t[:, i * LANES : (i + 1) * LANES]
+        gfold[pl.ds(pl.multiple_of(c * rows + part * half, half), half), :] = fold
+
+    def gain_send():
+        lanes = pl.ds(pl.multiple_of((h * 4 + y) * pair, pair), pair)
+        gall[f] = jnp.sum(gfold[...].T, axis=0, keepdims=True) / gain[0:1, lanes]
+        for s in range(1, size):
+            send(gall.at[f], gall.at[f], gg_s.at[s], gg_r.at[s], f_peer[s])
+
+    def gain_end():
+        for s in range(1, size):
+            landed(gall.at[lax.rem(f + size - s, size)], gg_s.at[s], gg_r.at[s], f_peer[s])
+        for j in range(chunks):
+            ggain_out[0:1, j * pair : (j + 1) * pair] = gall[2 * j] + gall[2 * j + 1]
 
     def chunk(d, r):
         j = mod4(h + d) * 4 + mod4(y + r)
         lanes = pl.ds(pl.multiple_of(j * pair, pair), pair)
         ng = lax.dot_general(kv[...], wbuf[lanes, :], (((1,), (1,)), ((), ())), preferred_element_type=F32)
         unit = x[:, lanes].astype(F32) * scale[...]
-        gs[pl.ds(j, 1), :] = jnp.sum(ng * unit, axis=0, keepdims=True)
         g = ng * gain[0:1, lanes]
         acc[...] += g * unit
         gb[:, lanes] = g
-
-    def plane(d):
-        for r in (0, 3, 1, 2):
-            as_wait(d, r)
-            chunk(d, r)
 
     def outer_first():
         loads[4].wait()
@@ -330,108 +434,45 @@
             nmom_out[:, at] = fresh
             npar_out[:, at] = par[:, at] - rate * (mean + NESTEROV_MU * fresh)
 
+    def az_fwd(k):
+        need(az_wait, k - 4)
+        az_send(k)
+
+    def ay_first(d, part):
+        need(az_wait, {(3, 0): 0, (1, 1): 1, (3, 1): 2, (1, 0): 3, (2, 0): 4, (2, 1): 5}[d, part])
+        for k in ((0, 3), (1, 2))[part]:
+            ay_send(d, k)
+
+    def ay_fwd(d, k):
+        need(ay_wait, d, k - 4)
+        ay_send(d, k)
+
+    def over(d, r):
+        if r == 0:
+            for k in {0: (), 1: (1, 3), 2: (4, 5), 3: (0, 2)}[d]:
+                need(az_wait, k)
+        else:
+            for k in {3: (0, 2), 1: (1, 3), 2: (4, 5)}[r]:
+                need(ay_wait, d, k)
+        as_send(d, r)
+
+    def mul(d, r):
+        need(as_wait, d, r)
+        chunk(d, r)
+
     acc[...] = jnp.zeros_like(acc)
-    norm(2)
-    norm(1)
-    landed(kv_sib, nt_s.at[4], nt_r.at[4], sib)
-    partial(2)
-    for k in (0, 1):
-        ay_wait(0, k)
-        ay_send(0, k + 4)
-    norm(3)
-    partial(1)
-    norm(0)
-    partial(3)
-    partial(0)
-    if outer:
-        outer_first()
-    ry_mid(2)
-    for k in (2, 3):
-        ay_wait(0, k)
-    as_send(0, 3)
-    as_send(0, 1)
-    loads[3].wait()
-    az_wait(0)
-    az_send(4)
-    ay_send(3, 0)
-    ay_send(3, 3)
-    az_wait(1)
-    az_send(5)
-    ay_send(1, 1)
-    ay_send(1, 2)
-    ry_mid(1)
-    ry_end(2)
-    rz_send(0)
-    rz_send(1)
-    if outer:
-        outer_second()
-    ry_mid(3)
-    ay_wait(0, 4)
-    ay_wait(0, 5)
-    as_send(0, 2)
-    ry_mid(0)
-    plane(0)
-    az_wait(2)
-    ay_send(3, 1)
-    ay_send(3, 2)
-    az_wait(3)
-    ay_send(1, 0)
-    ay_send(1, 3)
-    as_send(3, 0)
-    as_send(1, 0)
-    ry_end(1)
-    rz_send(2)
-    ry_end(3)
-    rz_send(3)
-    if outer:
-        outer_third()
-    rz_mid(0)
-    rz_mid(1)
-    ry_end(0)
-    az_wait(4)
-    ay_send(2, 0)
-    ay_send(2, 3)
-    az_wait(5)
-    ay_send(2, 1)
-    ay_send(2, 2)
-    as_send(2, 0)
-    for k in (0, 1):
-        ay_wait(3, k)
-        ay_send(3, k + 4)
-    for k in (0, 1):
-        ay_wait(1, k)
-        ay_send(1, k + 4)
-    if outer:
-        outer_last()
-    for d in (3, 1):
-        for k in (2, 3):
-            ay_wait(d, k)
-        as_send(d, 3)
-        as_send(d, 1)
-    for k in (0, 1):
-        ay_wait(2, k)
-        ay_send(2, k + 4)
-    for d in (3, 1):
-        for k in (4, 5):
-            ay_wait(d, k)
-        as_send(d, 2)
-        plane(d)
-    for k in (2, 3):
-        ay_wait(2, k)
-    as_send(2, 3)
-    as_send(2, 1)
-    for k in (4, 5):
-        ay_wait(2, k)
-    as_send(2, 2)
-    plane(2)
-
-    send(gs, gsib, gg_s.at[0], gg_r.at[0], sib)
+    gfold[...] = jnp.zeros_like(gfold)
+    kv_here = lambda: landed(kv_sib, nt_s.at[4], nt_r.at[4], sib)
+    tasks = dict(
+        norm=norm, kv_here=kv_here, partial=partial, az_fwd=az_fwd, ay_first=ay_first, ay_fwd=ay_fwd, over=over,
+        mul=mul, ry_mid=ry_mid, ry_end=ry_end, rz_send=rz_send, rz_mid=rz_mid, rz_end=rz_end, gain_send=gain_send,
+        outer_first=outer_first, outer_second=outer_second, outer_third=outer_third, outer_last=outer_last,
+    )
+    for name, *key in ORDER:
+        if outer or not name.startswith("outer"):
+            tasks[name](*key)
     inner = jnp.sum(acc[...], axis=-1, keepdims=True) * (1.0 / feat)
     acc[...] = jnp.broadcast_to(inner, acc.shape)
-    landed(gsib, gg_s.at[0], gg_r.at[0], sib)
-    gy[y] = gs[...] + gsib[...]
-    for s in (1, -1, 2):
-        send(gy.at[y], gy.at[y], gg_s.at[2 + s], gg_r.at[2 + s], y_peer[s])
 
     outs = []
     block = min(64, tok)
@@ -449,24 +490,35 @@
 
     n_final = tok // block
     for i in range(n_final):
-        if i == n_final // 2:
-            for s in (1, -1, 2):
-                landed(gy.at[mod4(y - s)], gg_s.at[2 + s], gg_r.at[2 + s], y_peer[s])
-            gz[h] = gy[0] + gy[1] + gy[2] + gy[3]
-            for s in (1, -1, 2):
-                send(gz.at[h], gz.at[h], gg_s.at[6 + s], gg_r.at[6 + s], h_peer[s])
         final(i)
 
-    rz_end()
-    for s in (1, -1, 2):
-        landed(gz.at[mod4(h - s)], gg_s.at[6 + s], gg_r.at[6 + s], h_peer[s])
-    total = gz[0] + gz[1] + gz[2] + gz[3]
-    for j in range(chunks):
-        ggain_out[0:1, j * pair : (j + 1) * pair] = total[j : j + 1, :]
+    for name, *key in LATE:
+        tasks[name](*key)
+    gain_end()
     for copy in pending:
         copy.wait_send()
     for out in outs:
         out.wait()
+
+
+def hand_on(*refs):
+    n = 5
+    ins, outs, stages, sems = refs[:n], refs[n : 2 * n], refs[2 * n : 3 * n], refs[3 * n]
+    loads, stores = [], []
+    for a, stage, b in zip(ins, stages, outs):
+        split = 4 if a.shape[0] >= 256 else 1
+        size = a.shape[0] // split
+        for i in range(split):
+            at = pl.ds(i * size, size)
+            loads.append(pltpu.make_async_copy(a.at[at, :], stage.at[at, :], sems.at[0, len(loads)]))
+            stores.append(pltpu.make_async_copy(stage.at[at, :], b.at[at, :], sems.at[1, len(stores)]))
+    for load in loads:
+        load.start()
+    for load, store in zip(loads, stores):
+        load.wait()
+        store.start()
+    for store in stores:
+        store.wait()
 
 
 def local(residual_in, norm_gain, kv_weight, kv_grad, outer_delta, outer_momentum, global_params, sync_index, outer=True):
@@ -479,7 +531,7 @@
     vmem = pl.BlockSpec(memory_space=pltpu.VMEM)
     dma = pltpu.SemaphoreType.DMA
     width = feat // 4
-    grad_kv, grad_gain, grad_input, new_params, new_momentum = pl.pallas_call(
+    results = pl.pallas_call(
         functools.partial(kernel, (tok, feat, kvw, outer)),
         out_shape=(
             jax.ShapeDtypeStruct((rows, kvw), BF16),
@@ -506,10 +558,8 @@
             pltpu.VMEM((tok, LANES), F32),
             pltpu.VMEM((tok, feat), F32),
             pltpu.VMEM((tok, feat), BF16),
-            pltpu.VMEM((chunks, pair), F32),
-            pltpu.VMEM((chunks, pair), F32),
-            pltpu.VMEM((4, chunks, pair), F32),
-            pltpu.VMEM((4, chunks, pair), F32),
+            pltpu.VMEM((pair, LANES), F32),
+            pltpu.VMEM((2 * chunks, 1, pair), F32),
             pltpu.VMEM((frag, feat), F32),
             pltpu.VMEM((frag, feat), F32),
             pltpu.VMEM((frag, feat), F32),
@@ -535,8 +585,8 @@
             dma((4,)),
             dma((2, 4)),
             dma((2, 4)),
-            dma((9,)),
-            dma((9,)),
+            dma((2 * chunks,)),
+            dma((2 * chunks,)),
         ],
         compiler_params=pltpu.CompilerParams(
             collective_id=0, has_side_effects=True, vmem_limit_bytes=56 * 1024 * 1024
@@ -551,6 +601,14 @@
         global_params,
         sync_index,
     )
+    grad_kv, grad_gain, grad_input, new_params, new_momentum = pl.pallas_call(
+        hand_on,
+        out_shape=tuple(jax.ShapeDtypeStruct(r.shape, r.dtype) for r in results),
+        in_specs=[any_space] * 5,
+        out_specs=(any_space,) * 5,
+        scratch_shapes=[pltpu.VMEM(r.shape, r.dtype) for r in results] + [dma((2, 8))],
+        compiler_params=pltpu.CompilerParams(vmem_limit_bytes=60 * 1024 * 1024),
+    )(*results)
     return (grad_kv[None], grad_gain, grad_input[None], new_params, new_momentum)
 
 

time: 83.6 us -> 75.4 us (0.902); the launches traced: 82.1 us -> 74.9 us
  local copies, waits for them, and re-layouts: 6.95 us -> 0 us
    unnamed x9 -> x0, local copies, waits for them, and re-layouts: 6.95 us -> none
    pallas_call x1, Pallas kernels: 73.8 us -> 71.2 us  [local(): pl.pallas_call(functools.partial(kernel, (tok, feat, kvw, outer)), out_sh...]
    pallas_call x0 -> x1, Pallas kernels: none -> 2.44 us  [local(): pl.pallas_call(hand_on, out_shape=tuple((jax.ShapeDtypeStruct(r.shape, r....]
where the time goes in v2:
time: 75.4 us; the launch traced here: 74.9 us
  Pallas kernels  73.6 us (98%)
  between operations  1.29 us (2%)
    pallas_call x1, Pallas kernels, local(): pl.pallas_call(functools.partial(kernel, (tok, feat, kvw, outer)), out_sh...  71.2 us
    pallas_call x1, Pallas kernels, local(): pl.pallas_call(hand_on, out_shape=tuple((jax.ShapeDtypeStruct(r.shape, r....  2.44 us

profile of v2, /device:TPU:1, one launch (start us, length us, event | category | flops | bytes accessed | tf_op | source)
XLA Modules:
  0.0 74.9 jit_solution(8445851217816997269)
XLA Ops:
  1.3 71.2 %shard_map.119 = (bf16[64,1024]{1,0:T(8,128)(2,1)}, f32[1,2048]{1,0:T(1,128)}, bf16[384,2048]{1,0:T(8,128)(2,1)}, f32[16,2048]{1,0:T(8,128)}, f32[16,2048]{1,0:T(8,128)}) custom-call(bf16[384,2048]{1,0:T(8,128)(2,1)} %bitcast.6, f32[1,2048]{1,0:T(1,128)} %gain_hbm.1, bf16[64,1024]{1,0:T(8,128)(2,1)} %bitcast.8, bf16[384,1024]{1,0:T(8,128)(2,1)} %bitcast.7, ...), custom_call_target="tpu_custom_call" | custom-call | tf_op jit(solution)/shard_map/pallas_call | solution.py:534
  72.4 2.4 %shard_map.120 = (bf16[64,1024]{1,0:T(8,128)(2,1)}, f32[1,2048]{1,0:T(1,128)}, bf16[384,2048]{1,0:T(8,128)(2,1)}, f32[16,2048]{1,0:T(8,128)}, f32[16,2048]{1,0:T(8,128)}) custom-call(bf16[64,1024]{1,0:T(8,128)(2,1)} %get-tuple-element.15.refs_0_, f32[1,2048]{1,0:T(1,128)} %get-tuple-element.16.refs_1_, bf16[384,2048]{1,0:T(8,128)(2,1)} %get-tuple-element.17.refs_2_, ...), custom_call_target="tpu_custom_call" | custom-call | tf_op jit(solution)/shard_map/pallas_call | solution.py:604

commit v3 on v2

--- a/solution.py
+++ b/solution.py
@@ -19,91 +19,101 @@
 ORDER = (
     ("norm", 2),
     ("norm", 1),
-    ("norm", 3),
+    ("mul", 0, 0),
     ("ay_fwd", 0, 4),
     ("ay_fwd", 0, 5),
     ("over", 0, 1),
     ("over", 0, 3),
     ("kv_here",),
     ("partial", 2),
+    ("outer_first",),
     ("partial", 1),
-    ("partial", 3),
-    ("outer_first",),
+    ("norm", 3),
     ("over", 0, 2),
-    ("mul", 0, 0),
     ("mul", 0, 1),
     ("mul", 0, 3),
+    ("outer_second",),
     ("mul", 0, 2),
-    ("outer_second",),
+    ("partial", 3),
+    ("ry_mid", 2, 0),
+    ("ry_mid", 2, 1),
+    ("norm", 0),
+    ("outer_third",),
     ("az_fwd", 4),
     ("az_fwd", 5),
-    ("ry_mid", 2, 0),
-    ("ry_mid", 2, 1),
     ("over", 1, 0),
-    ("outer_third",),
     ("over", 3, 0),
     ("ry_mid", 1, 0),
     ("ry_mid", 1, 1),
+    ("partial", 0),
+    ("outer_last",),
+    ("ry_mid", 3, 1),
     ("ry_mid", 3, 0),
-    ("ry_mid", 3, 1),
+    ("mul", 1, 0),
+    ("mul", 3, 0),
+    ("ry_end", 2, 0),
+    ("rz_send", 0),
+    ("ry_end", 2, 1),
+    ("rz_send", 1),
+    ("ay_first", 2, 1),
+    ("over", 2, 0),
+    ("ry_end", 1, 0),
+    ("ry_end", 1, 1),
     ("ay_first", 3, 0),
     ("ay_first", 1, 1),
-    ("outer_last",),
-    ("ry_end", 2, 1),
-    ("ry_end", 2, 0),
+    ("rz_send", 2),
+    ("gain_part", 1, 0),
+    ("gain_part", 1, 1),
+    ("gain_part", 2, 0),
+    ("ry_mid", 0, 0),
+    ("ry_mid", 0, 1),
+    ("gain_part", 2, 1),
+    ("mul", 2, 0),
+    ("ry_end", 3, 0),
+    ("ay_first", 2, 0),
+    ("ay_first", 3, 1),
+    ("rz_send", 3),
+    ("ry_end", 3, 1),
+    ("gain_part", 3, 0),
+    ("gain_part", 3, 1),
+    ("rz_mid", 1),
+    ("ay_fwd", 2, 5),
     ("ay_first", 1, 0),
-    ("rz_send", 0),
-    ("rz_send", 1),
-    ("mul", 3, 0),
-    ("ry_end", 1, 0),
-    ("ry_end", 1, 1),
-    ("rz_send", 2),
-    ("ay_first", 3, 1),
-    ("over", 2, 0),
-    ("ry_end", 3, 0),
-    ("ry_end", 3, 1),
-    ("ay_fwd", 1, 5),
+    ("rz_mid", 0),
     ("ay_fwd", 3, 4),
-    ("norm", 0),
-    ("ay_fwd", 1, 4),
-    ("over", 1, 1),
-    ("over", 1, 3),
-    ("ay_first", 2, 0),
-    ("ay_first", 2, 1),
-    ("rz_send", 3),
-    ("mul", 1, 0),
-    ("mul", 2, 0),
+    ("ry_end", 0, 0),
+    ("gain_part", 0, 0),
+    ("ry_end", 0, 1),
+    ("gain_part", 0, 1),
+    ("gain_send",),
+    ("ay_fwd", 2, 4),
+    ("over", 2, 3),
     ("over", 3, 3),
+    ("over", 2, 1),
     ("ay_fwd", 3, 5),
     ("over", 3, 1),
-    ("mul", 1, 1),
-    ("partial", 0),
-    ("rz_mid", 1),
-    ("mul", 1, 3),
+    ("ay_fwd", 1, 4),
+    ("ay_fwd", 1, 5),
+    ("over", 1, 3),
+    ("mul", 2, 3),
+    ("over", 1, 1),
+    ("mul", 2, 1),
     ("mul", 3, 1),
     ("mul", 3, 3),
-    ("rz_mid", 0),
-    ("ay_fwd", 2, 5),
-    ("over", 2, 1),
+    ("mul", 1, 3),
+    ("over", 2, 2),
+    ("over", 3, 2),
+    ("mul", 1, 1),
+    ("gain_pass",),
     ("over", 1, 2),
-    ("ay_fwd", 2, 4),
-    ("over", 2, 3),
-    ("over", 3, 2),
-    ("mul", 2, 1),
+    ("mul", 2, 2),
+    ("mul", 3, 2),
+    ("rz_end", 0),
+    ("rz_end", 1),
     ("mul", 1, 2),
-    ("mul", 2, 3),
-    ("ry_mid", 0, 0),
-    ("ry_mid", 0, 1),
-    ("mul", 3, 2),
-    ("over", 2, 2),
-    ("mul", 2, 2),
-    ("ry_end", 0, 0),
-    ("ry_end", 0, 1),
 )
 LATE = (
-    ("rz_end", 0),
-    ("rz_end", 1),
-    ("gain_send",),
+    ("gain_end",),
 )
 
 
@@ -117,11 +127,11 @@
     mom_hbm,
     par_hbm,
     sync_ref,
-    gkv_out,
-    ggain_out,
+    gkv_hbm,
+    ggain_hbm,
     gin_hbm,
-    npar_out,
-    nmom_out,
+    npar_hbm,
+    nmom_hbm,
     x,
     gain,
     wbuf,
@@ -137,7 +147,12 @@
     acc,
     gb,
     obuf,
+    gkv,
+    ggain,
+    npar,
+    nmom,
     gfold,
+    gz,
     gall,
     delta,
     mom,
@@ -193,9 +208,9 @@
     l_peer = {s: {"rep": mod4(zl + s) * 4 + xx} for s in (1, 2, 3)}
 
     barrier = pltpu.get_barrier_semaphore()
-    size = 2 * chunks
-    f_peer = {s: {"fsdp": lax.rem(f + s, size)} for s in range(1, size)}
-    peers = list(f_peer.values())
+    near = [sib] + [inside(h, mod4(y + s), cc) for s in (1, -1, 2) for cc in (c, 1 - c)]
+    near_from = near[:1] + [inside(h, mod4(y - s), cc) for s in (1, -1, 2) for cc in (c, 1 - c)]
+    peers = near + list(h_peer.values())
     if outer:
         peers += list(x_peer.values()) + list(l_peer.values())
     for peer in peers:
@@ -220,6 +235,13 @@
     for i in (3, 1, 0, 2, 4, 5, 6):
         loads[i].start()
 
+    outs = []
+
+    def give(src, dst):
+        out = pltpu.make_async_copy(src, dst, sem_out.at[len(outs)])
+        out.start()
+        outs.append(out)
+
     pending = []
 
     def send(src, dst, ssem, rsem, peer):
@@ -366,24 +388,42 @@
         for k in ENDS[part]:
             need(rz_wait, k)
             t = t + zbuf[k].astype(F32)
-        gkv_out[part * half : (part + 1) * half, :] = t.astype(BF16)
-        t = t * blk(h, y, c, part)[...].astype(F32)
+        gkv[part * half : (part + 1) * half, :] = t.astype(BF16)
+        give(gkv.at[part * half : (part + 1) * half, :], gkv_hbm.at[part * half : (part + 1) * half, :])
+
+    def gain_part(d, part):
+        for k in {0: (), 1: (1, 3), 2: (4, 5), 3: (0, 2)}[d]:
+            need(az_wait, k)
+        p = mod4(h + d)
+        t = yb[d, part].astype(F32) * blk(p, y, c, part)[...].astype(F32)
         fold = t[:, :LANES]
         for i in range(1, kvw // LANES):
             fold = fold + t[:, i * LANES : (i + 1) * LANES]
-        gfold[pl.ds(pl.multiple_of(c * rows + part * half, half), half), :] = fold
+        gfold[p, pl.ds(pl.multiple_of(c * rows + part * half, half), half), :] = fold
 
     def gain_send():
-        lanes = pl.ds(pl.multiple_of((h * 4 + y) * pair, pair), pair)
-        gall[f] = jnp.sum(gfold[...].T, axis=0, keepdims=True) / gain[0:1, lanes]
-        for s in range(1, size):
-            send(gall.at[f], gall.at[f], gg_s.at[s], gg_r.at[s], f_peer[s])
+        for p in range(4):
+            gz[h, p] = jnp.sum(gfold[p].T, axis=0, keepdims=True)
+        for s in (1, -1, 2):
+            send(gz.at[h], gz.at[h], gg_s.at[8 + s], gg_r.at[8 + s], h_peer[s])
+
+    def gain_pass():
+        for s in (1, -1, 2):
+            landed(gz.at[mod4(h - s)], gg_s.at[8 + s], gg_r.at[8 + s], h_peer[s])
+        mine = y * 2 + c
+        for p in range(4):
+            gall[mine, p] = gz[0, p] + gz[1, p] + gz[2, p] + gz[3, p]
+        for i, peer in enumerate(near):
+            send(gall.at[mine], gall.at[mine], gg_s.at[i], gg_r.at[i], peer)
 
     def gain_end():
-        for s in range(1, size):
-            landed(gall.at[lax.rem(f + size - s, size)], gg_s.at[s], gg_r.at[s], f_peer[s])
-        for j in range(chunks):
-            ggain_out[0:1, j * pair : (j + 1) * pair] = gall[2 * j] + gall[2 * j + 1]
+        for i, peer in enumerate(near_from):
+            landed(gall.at[lax.rem(peer["fsdp"], 8)], gg_s.at[i], gg_r.at[i], near[i])
+        for p in range(4):
+            for q in range(4):
+                lanes = slice((p * 4 + q) * pair, (p * 4 + q + 1) * pair)
+                ggain[0:1, lanes] = (gall[2 * q, p] + gall[2 * q + 1, p]) / gain[0:1, lanes]
+        give(ggain, ggain_hbm)
 
     def chunk(d, r):
         j = mod4(h + d) * 4 + mod4(y + r)
@@ -431,8 +471,10 @@
             at = slice(i * width, (i + 1) * width)
             mean = dt[i].astype(F32) * (1.0 / 16)
             fresh = NESTEROV_MU * mom[:, at] + mean
-            nmom_out[:, at] = fresh
-            npar_out[:, at] = par[:, at] - rate * (mean + NESTEROV_MU * fresh)
+            nmom[:, at] = fresh
+            npar[:, at] = par[:, at] - rate * (mean + NESTEROV_MU * fresh)
+        give(nmom, nmom_hbm)
+        give(npar, npar_hbm)
 
     def az_fwd(k):
         need(az_wait, k - 4)
@@ -465,7 +507,8 @@
     kv_here = lambda: landed(kv_sib, nt_s.at[4], nt_r.at[4], sib)
     tasks = dict(
         norm=norm, kv_here=kv_here, partial=partial, az_fwd=az_fwd, ay_first=ay_first, ay_fwd=ay_fwd, over=over,
-        mul=mul, ry_mid=ry_mid, ry_end=ry_end, rz_send=rz_send, rz_mid=rz_mid, rz_end=rz_end, gain_send=gain_send,
+        mul=mul, ry_mid=ry_mid, ry_end=ry_end, rz_send=rz_send, rz_mid=rz_mid, rz_end=rz_end, gain_part=gain_part,
+        gain_send=gain_send, gain_pass=gain_pass, gain_end=gain_end,
         outer_first=outer_first, outer_second=outer_second, outer_third=outer_third, outer_last=outer_last,
     )
     for name, *key in ORDER:
@@ -474,7 +517,6 @@
     inner = jnp.sum(acc[...], axis=-1, keepdims=True) * (1.0 / feat)
     acc[...] = jnp.broadcast_to(inner, acc.shape)
 
-    outs = []
     block = min(64, tok)
 
     def final(i):
@@ -484,17 +526,12 @@
             lanes = slice(j * pair, (j + 1) * pair)
             unit = x[at, lanes].astype(F32) * sc
             obuf[at, lanes] = (sc * (gb[at, lanes] - unit * inn)).astype(BF16)
-        out = pltpu.make_async_copy(obuf.at[at, :], gin_hbm.at[at, :], sem_out.at[i])
-        out.start()
-        outs.append(out)
-
-    n_final = tok // block
-    for i in range(n_final):
+        give(obuf.at[at, :], gin_hbm.at[at, :])
+
+    for i in range(tok // block):
         final(i)
-
     for name, *key in LATE:
         tasks[name](*key)
-    gain_end()
     for copy in pending:
         copy.wait_send()
     for out in outs:
@@ -528,7 +565,6 @@
     half, pair = rows // 2, 2 * rows
     chunks = feat // pair
     any_space = pl.BlockSpec(memory_space=pl.ANY)
-    vmem = pl.BlockSpec(memory_space=pltpu.VMEM)
     dma = pltpu.SemaphoreType.DMA
     width = feat // 4
     results = pl.pallas_call(
@@ -541,7 +577,7 @@
             jax.ShapeDtypeStruct((frag, feat), F32),
         ),
         in_specs=[any_space] * 7 + [pl.BlockSpec(memory_space=pltpu.SMEM)],
-        out_specs=(vmem, vmem, any_space, vmem, vmem),
+        out_specs=(any_space,) * 5,
         scratch_shapes=[
             pltpu.VMEM((tok, feat), BF16),
             pltpu.VMEM((1, feat), F32),
@@ -558,8 +594,13 @@
             pltpu.VMEM((tok, LANES), F32),
             pltpu.VMEM((tok, feat), F32),
             pltpu.VMEM((tok, feat), BF16),
-            pltpu.VMEM((pair, LANES), F32),
-            pltpu.VMEM((2 * chunks, 1, pair), F32),
+            pltpu.VMEM((rows, kvw), BF16),
+            pltpu.VMEM((1, feat), F32),
+            pltpu.VMEM((frag, feat), F32),
+            pltpu.VMEM((frag, feat), F32),
+            pltpu.VMEM((4, pair, LANES), F32),
+            pltpu.VMEM((4, 4, 1, LANES), F32),
+            pltpu.VMEM((8, 4, 1, LANES), F32),
             pltpu.VMEM((frag, feat), F32),
             pltpu.VMEM((frag, feat), F32),
             pltpu.VMEM((frag, feat), F32),
@@ -568,7 +609,7 @@
             pltpu.VMEM((4, frag, width), BF16),
             pltpu.VMEM((4, frag, width), BF16),
             dma((7,)),
-            dma((tok // min(64, tok),)),
+            dma((tok // min(64, tok) + 5,)),
             dma((6,)),
             dma((6,)),
             dma((4, 6)),
@@ -585,8 +626,8 @@
             dma((4,)),
             dma((2, 4)),
             dma((2, 4)),
-            dma((2 * chunks,)),
-            dma((2 * chunks,)),
+            dma((11,)),
+            dma((11,)),
         ],
         compiler_params=pltpu.CompilerParams(
             collective_id=0, has_side_effects=True, vmem_limit_bytes=56 * 1024 * 1024

time: 75.4 us -> 71.8 us (0.952)
  Pallas kernels: 73.6 us -> 70.3 us
    pallas_call x1, Pallas kernels: 71.2 us -> 67.8 us  [local(): pl.pallas_call(functools.partial(kernel, (tok, feat, kvw, outer)), out_sh...]
where the time goes in v3:
time: 71.8 us; the launch traced here: 71.6 us
  Pallas kernels  70.3 us (98%)
  between operations  1.29 us (2%)
    pallas_call x1, Pallas kernels, local(): pl.pallas_call(functools.partial(kernel, (tok, feat, kvw, outer)), out_sh...  67.8 us
    pallas_call x1, Pallas kernels, local(): pl.pallas_call(hand_on, out_shape=tuple((jax.ShapeDtypeStruct(r.shape, r....  2.44 us

profile of v3, /device:TPU:1, one launch (start us, length us, event | category | flops | bytes accessed | tf_op | source)
XLA Modules:
  0.0 71.6 jit_solution(6259172723765768757)
XLA Ops:
  1.3 67.8 %shard_map.119 = (bf16[64,1024]{1,0:T(8,128)(2,1)}, f32[1,2048]{1,0:T(1,128)}, bf16[384,2048]{1,0:T(8,128)(2,1)}, f32[16,2048]{1,0:T(8,128)}, f32[16,2048]{1,0:T(8,128)}) custom-call(bf16[384,2048]{1,0:T(8,128)(2,1)} %bitcast.6, f32[1,2048]{1,0:T(1,128)} %gain_hbm.1, bf16[64,1024]{1,0:T(8,128)(2,1)} %bitcast.8, bf16[384,1024]{1,0:T(8,128)(2,1)} %bitcast.7, ...), custom_call_target="tpu_custom_call" | custom-call | tf_op jit(solution)/shard_map/pallas_call | solution.py:570
  69.1 2.4 %shard_map.120 = (bf16[64,1024]{1,0:T(8,128)(2,1)}, f32[1,2048]{1,0:T(1,128)}, bf16[384,2048]{1,0:T(8,128)(2,1)}, f32[16,2048]{1,0:T(8,128)}, f32[16,2048]{1,0:T(8,128)}) custom-call(bf16[64,1024]{1,0:T(8,128)(2,1)} %get-tuple-element.15.refs_0_, f32[1,2048]{1,0:T(1,128)} %get-tuple-element.16.refs_1_, bf16[384,2048]{1,0:T(8,128)(2,1)} %get-tuple-element.17.refs_2_, ...), custom_call_target="tpu_custom_call" | custom-call | tf_op jit(solution)/shard_map/pallas_call | solution.py:645

commit v4 on v3

--- a/solution.py
+++ b/solution.py
@@ -19,6 +19,8 @@
 ORDER = (
     ("norm", 2),
     ("norm", 1),
+    ("norm", 3),
+    ("norm", 0),
     ("mul", 0, 0),
     ("ay_fwd", 0, 4),
     ("ay_fwd", 0, 5),
@@ -28,92 +30,90 @@
     ("partial", 2),
     ("outer_first",),
     ("partial", 1),
-    ("norm", 3),
     ("over", 0, 2),
+    ("partial", 3),
+    ("partial", 0),
+    ("outer_second",),
     ("mul", 0, 1),
+    ("mul", 0, 2),
     ("mul", 0, 3),
-    ("outer_second",),
-    ("mul", 0, 2),
-    ("partial", 3),
-    ("ry_mid", 2, 0),
-    ("ry_mid", 2, 1),
-    ("norm", 0),
-    ("outer_third",),
     ("az_fwd", 4),
     ("az_fwd", 5),
     ("over", 1, 0),
     ("over", 3, 0),
-    ("ry_mid", 1, 0),
-    ("ry_mid", 1, 1),
-    ("partial", 0),
-    ("outer_last",),
-    ("ry_mid", 3, 1),
-    ("ry_mid", 3, 0),
+    ("ry_mid", 2, 0),
+    ("ry_mid", 2, 1),
+    ("ay_first", 1, 1),
+    ("ay_first", 1, 0),
+    ("ay_first", 3, 0),
+    ("ay_first", 3, 1),
+    ("outer_third",),
     ("mul", 1, 0),
     ("mul", 3, 0),
+    ("outer_last",),
+    ("ry_mid", 1, 1),
+    ("ry_mid", 1, 0),
+    ("ay_first", 2, 0),
+    ("ay_first", 2, 1),
+    ("over", 2, 0),
+    ("mul", 2, 0),
+    ("ry_mid", 3, 0),
+    ("ry_mid", 3, 1),
+    ("ry_mid", 0, 1),
+    ("ry_mid", 0, 0),
     ("ry_end", 2, 0),
     ("rz_send", 0),
     ("ry_end", 2, 1),
     ("rz_send", 1),
-    ("ay_first", 2, 1),
-    ("over", 2, 0),
+    ("ay_fwd", 1, 4),
+    ("ay_fwd", 1, 5),
+    ("ay_fwd", 3, 4),
+    ("ay_fwd", 3, 5),
+    ("over", 1, 1),
+    ("over", 1, 3),
+    ("over", 3, 1),
+    ("over", 3, 3),
+    ("gain_part", 2, 0),
+    ("gain_part", 2, 1),
+    ("mul", 1, 1),
+    ("mul", 1, 3),
+    ("mul", 3, 1),
+    ("mul", 3, 3),
+    ("ry_end", 1, 1),
+    ("rz_send", 2),
     ("ry_end", 1, 0),
-    ("ry_end", 1, 1),
-    ("ay_first", 3, 0),
-    ("ay_first", 1, 1),
-    ("rz_send", 2),
     ("gain_part", 1, 0),
+    ("ay_fwd", 2, 4),
+    ("ay_fwd", 2, 5),
+    ("over", 2, 1),
+    ("over", 2, 3),
     ("gain_part", 1, 1),
-    ("gain_part", 2, 0),
-    ("ry_mid", 0, 0),
-    ("ry_mid", 0, 1),
-    ("gain_part", 2, 1),
-    ("mul", 2, 0),
     ("ry_end", 3, 0),
-    ("ay_first", 2, 0),
-    ("ay_first", 3, 1),
     ("rz_send", 3),
     ("ry_end", 3, 1),
     ("gain_part", 3, 0),
     ("gain_part", 3, 1),
-    ("rz_mid", 1),
-    ("ay_fwd", 2, 5),
-    ("ay_first", 1, 0),
-    ("rz_mid", 0),
-    ("ay_fwd", 3, 4),
     ("ry_end", 0, 0),
+    ("ry_end", 0, 1),
     ("gain_part", 0, 0),
-    ("ry_end", 0, 1),
     ("gain_part", 0, 1),
     ("gain_send",),
-    ("ay_fwd", 2, 4),
-    ("over", 2, 3),
-    ("over", 3, 3),
-    ("over", 2, 1),
-    ("ay_fwd", 3, 5),
-    ("over", 3, 1),
-    ("ay_fwd", 1, 4),
-    ("ay_fwd", 1, 5),
-    ("over", 1, 3),
+    ("mul", 2, 1),
     ("mul", 2, 3),
-    ("over", 1, 1),
-    ("mul", 2, 1),
-    ("mul", 3, 1),
-    ("mul", 3, 3),
-    ("mul", 1, 3),
+    ("over", 1, 2),
+    ("over", 3, 2),
     ("over", 2, 2),
-    ("over", 3, 2),
-    ("mul", 1, 1),
+    ("rz_mid", 1),
+    ("mul", 1, 2),
+    ("mul", 3, 2),
+    ("rz_mid", 0),
+    ("mul", 2, 2),
+)
+LATE = (
     ("gain_pass",),
-    ("over", 1, 2),
-    ("mul", 2, 2),
-    ("mul", 3, 2),
+    ("gain_end",),
     ("rz_end", 0),
     ("rz_end", 1),
-    ("mul", 1, 2),
-)
-LATE = (
-    ("gain_end",),
 )
 
 
@@ -127,11 +127,11 @@
     mom_hbm,
     par_hbm,
     sync_ref,
-    gkv_hbm,
-    ggain_hbm,
-    gin_hbm,
-    npar_hbm,
-    nmom_hbm,
+    gkv,
+    ggain,
+    obuf,
+    npar,
+    nmom,
     x,
     gain,
     wbuf,
@@ -146,11 +146,6 @@
     scale,
     acc,
     gb,
-    obuf,
-    gkv,
-    ggain,
-    npar,
-    nmom,
     gfold,
     gz,
     gall,
@@ -162,7 +157,6 @@
     dz,
     dt,
     sem_in,
-    sem_out,
     az_s,
     az_r,
     ay_s,
@@ -235,13 +229,6 @@
     for i in (3, 1, 0, 2, 4, 5, 6):
         loads[i].start()
 
-    outs = []
-
-    def give(src, dst):
-        out = pltpu.make_async_copy(src, dst, sem_out.at[len(outs)])
-        out.start()
-        outs.append(out)
-
     pending = []
 
     def send(src, dst, ssem, rsem, peer):
@@ -389,7 +376,6 @@
             need(rz_wait, k)
             t = t + zbuf[k].astype(F32)
         gkv[part * half : (part + 1) * half, :] = t.astype(BF16)
-        give(gkv.at[part * half : (part + 1) * half, :], gkv_hbm.at[part * half : (part + 1) * half, :])
 
     def gain_part(d, part):
         for k in {0: (), 1: (1, 3), 2: (4, 5), 3: (0, 2)}[d]:
@@ -423,7 +409,6 @@
             for q in range(4):
                 lanes = slice((p * 4 + q) * pair, (p * 4 + q + 1) * pair)
                 ggain[0:1, lanes] = (gall[2 * q, p] + gall[2 * q + 1, p]) / gain[0:1, lanes]
-        give(ggain, ggain_hbm)
 
     def chunk(d, r):
         j = mod4(h + d) * 4 + mod4(y + r)
@@ -473,8 +458,6 @@
             fresh = NESTEROV_MU * mom[:, at] + mean
             nmom[:, at] = fresh
             npar[:, at] = par[:, at] - rate * (mean + NESTEROV_MU * fresh)
-        give(nmom, nmom_hbm)
-        give(npar, npar_hbm)
 
     def az_fwd(k):
         need(az_wait, k - 4)
@@ -526,7 +509,6 @@
             lanes = slice(j * pair, (j + 1) * pair)
             unit = x[at, lanes].astype(F32) * sc
             obuf[at, lanes] = (sc * (gb[at, lanes] - unit * inn)).astype(BF16)
-        give(obuf.at[at, :], gin_hbm.at[at, :])
 
     for i in range(tok // block):
         final(i)
@@ -534,28 +516,22 @@
         tasks[name](*key)
     for copy in pending:
         copy.wait_send()
-    for out in outs:
-        out.wait()
 
 
 def hand_on(*refs):
-    n = 5
-    ins, outs, stages, sems = refs[:n], refs[n : 2 * n], refs[2 * n : 3 * n], refs[3 * n]
-    loads, stores = [], []
-    for a, stage, b in zip(ins, stages, outs):
+    n = len(refs) // 2
+    ins, outs, sems = refs[:n], refs[n : 2 * n], refs[2 * n]
+    copies = []
+    for a, b in zip(ins, outs):
         split = 4 if a.shape[0] >= 256 else 1
         size = a.shape[0] // split
         for i in range(split):
             at = pl.ds(i * size, size)
-            loads.append(pltpu.make_async_copy(a.at[at, :], stage.at[at, :], sems.at[0, len(loads)]))
-            stores.append(pltpu.make_async_copy(stage.at[at, :], b.at[at, :], sems.at[1, len(stores)]))
-    for load in loads:
-        load.start()
-    for load, store in zip(loads, stores):
-        load.wait()
-        store.start()
-    for store in stores:
-        store.wait()
+            copies.append(pltpu.make_async_copy(a.at[at, :], b.at[at, :], sems.at[len(copies)]))
+    for copy in copies:
+        copy.start()
+    for copy in copies:
+        copy.wait()
 
 
 def local(residual_in, norm_gain, kv_weight, kv_grad, outer_delta, outer_momentum, global_params, sync_index, outer=True):
@@ -570,14 +546,14 @@
     results = pl.pallas_call(
         functools.partial(kernel, (tok, feat, kvw, outer)),
         out_shape=(
-            jax.ShapeDtypeStruct((rows, kvw), BF16),
-            jax.ShapeDtypeStruct((1, feat), F32),
-            jax.ShapeDtypeStruct((tok, feat), BF16),
-            jax.ShapeDtypeStruct((frag, feat), F32),
-            jax.ShapeDtypeStruct((frag, feat), F32),
+            pltpu.VMEM((rows, kvw), BF16),
+            pltpu.VMEM((1, feat), F32),
+            pltpu.VMEM((tok, feat), BF16),
+            pltpu.VMEM((frag, feat), F32),
+            pltpu.VMEM((frag, feat), F32),
         ),
         in_specs=[any_space] * 7 + [pl.BlockSpec(memory_space=pltpu.SMEM)],
-        out_specs=(any_space,) * 5,
+        out_specs=(pl.BlockSpec(memory_space=pltpu.VMEM),) * 5,
         scratch_shapes=[
             pltpu.VMEM((tok, feat), BF16),
             pltpu.VMEM((1, feat), F32),
@@ -593,11 +569,6 @@
             pltpu.VMEM((tok, LANES), F32),
             pltpu.VMEM((tok, LANES), F32),
             pltpu.VMEM((tok, feat), F32),
-            pltpu.VMEM((tok, feat), BF16),
-            pltpu.VMEM((rows, kvw), BF16),
-            pltpu.VMEM((1, feat), F32),
-            pltpu.VMEM((frag, feat), F32),
-            pltpu.VMEM((frag, feat), F32),
             pltpu.VMEM((4, pair, LANES), F32),
             pltpu.VMEM((4, 4, 1, LANES), F32),
             pltpu.VMEM((8, 4, 1, LANES), F32),
@@ -609,7 +580,6 @@
             pltpu.VMEM((4, frag, width), BF16),
             pltpu.VMEM((4, frag, width), BF16),
             dma((7,)),
-            dma((tok // min(64, tok) + 5,)),
             dma((6,)),
             dma((6,)),
             dma((4, 6)),
@@ -630,7 +600,7 @@
             dma((11,)),
         ],
         compiler_params=pltpu.CompilerParams(
-            collective_id=0, has_side_effects=True, vmem_limit_bytes=56 * 1024 * 1024
+            collective_id=0, has_side_effects=True, vmem_limit_bytes=60 * 1024 * 1024
         ),
     )(
         residual_in[0],
@@ -645,10 +615,10 @@
     grad_kv, grad_gain, grad_input, new_params, new_momentum = pl.pallas_call(
         hand_on,
         out_shape=tuple(jax.ShapeDtypeStruct(r.shape, r.dtype) for r in results),
-        in_specs=[any_space] * 5,
+        in_specs=[pl.BlockSpec(memory_space=pltpu.VMEM)] * 5,
         out_specs=(any_space,) * 5,
-        scratch_shapes=[pltpu.VMEM(r.shape, r.dtype) for r in results] + [dma((2, 8))],
-        compiler_params=pltpu.CompilerParams(vmem_limit_bytes=60 * 1024 * 1024),
+        scratch_shapes=[dma((8,))],
+        compiler_params=pltpu.CompilerParams(vmem_limit_bytes=8 * 1024 * 1024),
     )(*results)
     return (grad_kv[None], grad_gain, grad_input[None], new_params, new_momentum)
 

time: 71.8 us -> 67 us (0.933)
  Pallas kernels: 70.3 us -> 65.5 us
    pallas_call x1, Pallas kernels: 67.8 us -> 64.2 us  [local(): pl.pallas_call(functools.partial(kernel, (tok, feat, kvw, outer)), out_sh...]
    pallas_call x1, Pallas kernels: 2.44 us -> 1.34 us  [local(): pl.pallas_call(hand_on, out_shape=tuple((jax.ShapeDtypeStruct(r.shape, r....]
where the time goes in v4:
time: 67 us; the launch traced here: 66.8 us
  Pallas kernels  65.5 us (98%)
  between operations  1.29 us (2%)
    pallas_call x1, Pallas kernels, local(): pl.pallas_call(functools.partial(kernel, (tok, feat, kvw, outer)), out_sh...  64.2 us

profile of v4, /device:TPU:1, one launch (start us, length us, event | category | flops | bytes accessed | tf_op | source)
XLA Modules:
  0.0 66.8 jit_solution(2125642517405358807)
XLA Ops:
  1.3 64.2 %shard_map.119 = (bf16[64,1024]{1,0:T(8,128)(2,1)S(1)}, f32[1,2048]{1,0:T(1,128)S(1)}, bf16[384,2048]{1,0:T(8,128)(2,1)S(1)}, f32[16,2048]{1,0:T(8,128)S(1)}, f32[16,2048]{1,0:T(8,128)S(1)}) custom-call(bf16[384,2048]{1,0:T(8,128)(2,1)} %bitcast.6, f32[1,2048]{1,0:T(1,128)} %gain_hbm.1, bf16[64,1024]{1,0:T(8,128)(2,1)} %bitcast.8, ...), custom_call_target="tpu_custom_call" | custom-call | tf_op jit(solution)/shard_map/pallas_call | solution.py:546
  65.5 1.3 %shard_map.120 = (bf16[64,1024]{1,0:T(8,128)(2,1)}, f32[1,2048]{1,0:T(1,128)}, bf16[384,2048]{1,0:T(8,128)(2,1)}, f32[16,2048]{1,0:T(8,128)}, f32[16,2048]{1,0:T(8,128)}) custom-call(bf16[64,1024]{1,0:T(8,128)(2,1)S(1)} %get-tuple-element.15.refs_0_, f32[1,2048]{1,0:T(1,128)S(1)} %get-tuple-element.16.refs_1_, ...), custom_call_target="tpu_custom_call" | custom-call | tf_op jit(solution)/shard_map/pallas_call | solution.py:615

commit v5 on v4

--- a/solution.py
+++ b/solution.py
@@ -47,10 +47,8 @@
     ("ay_first", 1, 0),
     ("ay_first", 3, 0),
     ("ay_first", 3, 1),
-    ("outer_third",),
     ("mul", 1, 0),
     ("mul", 3, 0),
-    ("outer_last",),
     ("ry_mid", 1, 1),
     ("ry_mid", 1, 0),
     ("ay_first", 2, 0),
@@ -61,6 +59,7 @@
     ("ry_mid", 3, 1),
     ("ry_mid", 0, 1),
     ("ry_mid", 0, 0),
+    ("outer_third",),
     ("ry_end", 2, 0),
     ("rz_send", 0),
     ("ry_end", 2, 1),
@@ -98,6 +97,7 @@
     ("gain_part", 0, 0),
     ("gain_part", 0, 1),
     ("gain_send",),
+    ("outer_last",),
     ("mul", 2, 1),
     ("mul", 2, 3),
     ("over", 1, 2),
@@ -111,9 +111,9 @@
 )
 LATE = (
     ("gain_pass",),
-    ("gain_end",),
     ("rz_end", 0),
     ("rz_end", 1),
+    ("gain_end",),
 )
 
 
@@ -204,9 +204,10 @@
     barrier = pltpu.get_barrier_semaphore()
     near = [sib] + [inside(h, mod4(y + s), cc) for s in (1, -1, 2) for cc in (c, 1 - c)]
     near_from = near[:1] + [inside(h, mod4(y - s), cc) for s in (1, -1, 2) for cc in (c, 1 - c)]
-    peers = near + list(h_peer.values())
+    peers = list(h_peer.values())
     if outer:
-        peers += list(x_peer.values()) + list(l_peer.values())
+        peers += list(l_peer.values()) + list(x_peer.values())
+    peers += near
     for peer in peers:
         pl.semaphore_signal(barrier, inc=1, device_id=peer, device_id_type=MESH)
 

time: 67 us -> 66.7 us (level)
  no operation moved by 1% of the time
where the time goes in v5:
time: 66.7 us; the launch traced here: 66.4 us
  Pallas kernels  65.1 us (98%)
  between operations  1.29 us (2%)
    pallas_call x1, Pallas kernels, local(): pl.pallas_call(functools.partial(kernel, (tok, feat, kvw, outer)), out_sh...  63.7 us
    pallas_call x1, Pallas kernels, local(): pl.pallas_call(hand_on, out_shape=tuple((jax.ShapeDtypeStruct(r.shape, r....  1.34 us

profile of v5, /device:TPU:1, one launch (start us, length us, event | category | flops | bytes accessed | tf_op | source)
XLA Modules:
  0.0 66.4 jit_solution(15550272606104720925)
XLA Ops:
  1.3 63.7 %shard_map.119 = (bf16[64,1024]{1,0:T(8,128)(2,1)S(1)}, f32[1,2048]{1,0:T(1,128)S(1)}, bf16[384,2048]{1,0:T(8,128)(2,1)S(1)}, f32[16,2048]{1,0:T(8,128)S(1)}, f32[16,2048]{1,0:T(8,128)S(1)}) custom-call(bf16[384,2048]{1,0:T(8,128)(2,1)} %bitcast.6, f32[1,2048]{1,0:T(1,128)} %gain_hbm.1, bf16[64,1024]{1,0:T(8,128)(2,1)} %bitcast.8, ...), custom_call_target="tpu_custom_call" | custom-call | tf_op jit(solution)/shard_map/pallas_call | solution.py:547
  65.0 1.3 %shard_map.120 = (bf16[64,1024]{1,0:T(8,128)(2,1)}, f32[1,2048]{1,0:T(1,128)}, bf16[384,2048]{1,0:T(8,128)(2,1)}, f32[16,2048]{1,0:T(8,128)}, f32[16,2048]{1,0:T(8,128)}) custom-call(bf16[64,1024]{1,0:T(8,128)(2,1)S(1)} %get-tuple-element.15.refs_0_, f32[1,2048]{1,0:T(1,128)S(1)} %get-tuple-element.16.refs_1_, ...), custom_call_target="tpu_custom_call" | custom-call | tf_op jit(solution)/shard_map/pallas_call | solution.py:616
